TPU v7x, 512 devices: a whole 4x4x16 slice. The times are simulated.
512 devices in a mesh: loop: 16 (over x, y_hi, core), out: 32 (over z, y_lo).
Axes of the slice: x: 4, y: 4 (y_hi: 2, y_lo: 2; y = y_hi * 2 + y_lo), z: 16, core: 2. Of those that a mesh axis runs over, the one named last changes fastest.
Arguments:
- activations: bfloat16 [10, 128, 8192], P(None, 'loop'), may hold values from -6 to 6
- out_grads: bfloat16 [10, 128, 28672], P(None, 'loop', 'out'), may hold values from -6 to 6
- token_counts: int32 [10], replicated, may hold values from 1 to 128, 800 in all
- basis_in: bfloat16 [8192, 8192], P('loop', 'out'), may hold values from -0.0625 to 0.0625
- basis_out: bfloat16 [28672, 14336], P('out', 'loop'), may hold values from -0.03125 to 0.03125
- eigenvalues: float32 [14336, 8192], P('loop', 'out'), may hold values from 0.05 to 5
Outputs:
- scaled_queries: bfloat16 [2, 14336, 8192], P(None, 'loop', 'out')
- scores: float32 [2, 8], replicated
Inputs may be any that keep to these rules, and one draw needn't show every extreme that they name: `token_counts`: the counts sum to exactly 800, and the largest count is exactly 128.
All inputs are finite; a program needn't handle non-finite values.
Results may differ from a plain program's by a relative error of at most 0.0057.
Values may be sent and summed in bfloat16 or wider, within the bound.
A program may use at most 128 MiB of HBM per device.

v0:
```python
import jax
import jax.numpy as jnp
from jax import lax
from jax.sharding import PartitionSpec as P

DIN = 8192
KS = 14336
QUERIES = 2
damping = 0.1


def body(activations, out_grads, token_counts, basis_in, basis_out, eigenvalues):
    examples, rows_here, din = activations.shape
    loop_count = lax.axis_size("loop")
    slots = rows_here * loop_count
    cols_in = basis_in.shape[1]
    cols_out = basis_out.shape[1]
    flat_act = activations.reshape(examples * rows_here, din)
    rotated = jnp.dot(
        flat_act,
        lax.all_gather(basis_in, "loop", axis=0, tiled=True),
        preferred_element_type=jnp.float32,
    )
    rotated = rotated.astype(jnp.bfloat16).reshape(examples, rows_here, cols_in)
    rot_act = lax.all_gather(rotated, "loop", axis=1, tiled=True)
    grads_all = lax.all_gather(out_grads, "loop", axis=1, tiled=True)
    flat_grads = grads_all.reshape(examples * slots, grads_all.shape[2])
    partial_grad = jnp.dot(flat_grads, basis_out, preferred_element_type=jnp.float32)
    rot_rows = lax.psum(partial_grad, "out").astype(jnp.bfloat16)
    positions = jnp.arange(slots, dtype=jnp.int32)
    rot_grad = rot_rows.reshape(examples, slots, cols_out)
    valid = (positions[None, :] < token_counts[:, None]).astype(jnp.bfloat16)
    masked = rot_act * valid[:, :, None]
    factor = 1.0 / slots**0.5
    grad_rot = (
        jnp.einsum("etc,etd->ecd", rot_grad, masked, preferred_element_type=jnp.float32) * factor
    )
    queries = QUERIES
    scaled = (grad_rot[:queries] / (eigenvalues + damping)[None]).astype(jnp.bfloat16)
    partial_scores = jnp.einsum(
        "qcd,fcd->qf",
        scaled.astype(jnp.float32),
        grad_rot[queries:],
        precision=lax.Precision.HIGHEST,
    )
    scores = lax.psum(partial_scores, ("loop", "out")) / (KS * DIN) ** 0.5
    return (scaled, scores)


def solution(mesh):
    return jax.shard_map(
        body,
        mesh=mesh,
        in_specs=(
            P(None, "loop", None),
            P(None, "loop", "out"),
            P(),
            P("loop", "out"),
            P("out", "loop"),
            P("loop", "out"),
        ),
        out_specs=(P(None, "loop", "out"), P()),
        check_vma=False,
    )
```

profile of v0, /device:TPU:1, one launch (start us, length us, event | category | flops | bytes accessed | tf_op | source)
XLA Modules:
  0.0 460.0 jit_solution(11219350362788644562)
XLA Ops:
  7.2 0.0 copy-start
  7.2 0.0 all-gather.3.cloned.1.call-start
  7.2 0.7 all-gather.3.cloned.1.call-update
  7.9 0.0 all-gather.5.cloned.1.call-start
  8.0 0.7 all-gather.5.cloned.1.call-update
  8.7 0.7 fusion.17
  9.4 1.3 broadcast_add_fusion
  10.7 70.9 %all-gather.3.cloned.1.call-done = bf16[10,128,896]{2,1,0:T(8,128)(2,1)} async-done(((bf16[10,8,896]{2,1,0:T(8,128)(2,1)}), bf16[10,128,896]{2,1,0:T(8,128)(2,1)}) %all-gather.3.cloned.1.call-update) | async-done | bytes 2293776 | tf_op jit(solution)/shard_map/all_gather | solution.py:26
  81.5 0.0 copy-done
  81.6 6.5 %fusion.18 = f32[1280,896]{1,0:T(8,128)} fusion(bf16[1280,896]{1,0:T(8,128)(2,1)} %bitcast.18, bf16[896,896]{1,0:T(8,128)(2,1)S(1)} %copy-done), kind=kOutput, calls=%fused_computation.17 | convolution fusion | flops 2055208960 | bytes 8486912 | tf_op jit(solution)/shard_map/dot_general | solution.py:28
  88.1 214.5 %all-reduce.1 = bf16[1280,896]{1,0:T(8,128)(2,1)} all-reduce(f32[1280,896]{1,0:T(8,128)} %fusion.18), channel_id=1, replica_groups=mesh['loop'=16,'out'=32] {'out'}, use_global_device_ids=true, to_apply=%region_0.0 | all-reduce | flops 1146880 | bytes 6881280 | tf_op jit(solution)/shard_map/psum | solution.py:29
  302.6 0.0 all-gather.5.cloned.1.call-done
  302.6 0.0 copy-start.1
  302.6 3.6 fusion.8
  306.1 31.7 %all_gather.11 = bf16[10,128,256]{2,1,0:T(8,128)(2,1)S(1)} all-gather(bf16[10,8,256]{2,1,0:T(8,128)(2,1)S(1)} %fusion.8), channel_id=1, replica_groups=mesh['loop'=16,'out'=32] {'loop'}, dimensions={1}, use_global_device_ids=true | all-gather | bytes 696320 | tf_op jit(solution)/shard_map/all_gather | solution.py:25
  337.8 0.0 copy-done.1
  337.8 1.4 broadcast_multiply_fusion
  339.3 0.5 slice.9
  339.8 0.2 fusion.2
  340.0 0.0 copy-start.2
  340.0 12.0 %fusion.11 = f32[2,8]{1,0:T(2,128)S(1)} fusion(f32[8,896,256]{2,1,0:T(8,128)S(1)} %slice.9, bf16[2,896,256]{2,1,0:T(8,128)(2,1)S(1)} %fusion.2), kind=kOutput, calls=%fused_computation.9 | convolution fusion | flops 44040192 | bytes 8257600 | tf_op jit(solution)/shard_map/qcd,fcd->qf/dot_general | solution.py:40
  352.0 0.0 copy-done.2
  352.0 100.6 %psum.15 = f32[2,8]{1,0:T(2,128)S(1)} all-reduce(f32[2,8]{1,0:T(2,128)S(1)} %fusion.11), channel_id=1, replica_groups=mesh['loop'=16,'out'=32] {'loop','out'}, use_global_device_ids=true, to_apply=%region_1.0 | all-reduce | flops 16 | bytes 128 | tf_op jit(solution)/shard_map/psum | solution.py:46
  452.6 0.6 broadcast_multiply_fusion.1
Async XLA Ops:
  7.2 74.4 %copy-start = (bf16[896,896]{1,0:T(8,128)(2,1)S(1)}, bf16[896,896]{1,0:T(8,128)(2,1)}, u32[]{:S(2)}) copy-start(bf16[896,896]{1,0:T(8,128)(2,1)} %param.10) | copy-start | bytes 4816900
  7.2 74.4 %all-gather.3.cloned.1.call-start = ((), (), s32[]{:S(2)}) async-start(), calls=%async_computation | async-start | bytes 2437120 | tf_op jit(solution)/shard_map/all_gather | solution.py:26
  7.9 294.6 %all-gather.5.cloned.1.call-start = ((), (), s32[]{:S(2)}) async-start(), calls=%async_computation.1 | async-start | bytes 4456448 | tf_op jit(solution)/shard_map/all_gather | solution.py:21
  302.6 35.2 %copy-start.1 = (bf16[1280,896]{1,0:T(8,128)(2,1)S(1)}, bf16[1280,896]{1,0:T(8,128)(2,1)}, u32[]{:S(2)}) copy-start(bf16[1280,896]{1,0:T(8,128)(2,1)} %all-reduce.1) | copy-start | bytes 6881284
  340.0 12.0 %copy-start.2 = (bf16[2,896,256]{2,1,0:T(8,128)(2,1)}, bf16[2,896,256]{2,1,0:T(8,128)(2,1)S(1)}, u32[]{:S(2)}) copy-start(bf16[2,896,256]{2,1,0:T(8,128)(2,1)S(1)} %fusion.2) | copy-start | bytes 2752516
Sparse Core Ops, SparseCore 0:
  11.4 70.1 all-gather.2
  84.8 97.8 all-gather.4
where the time goes:
time: 460 us
  blocking collectives  347 us (75%)
  waiting for transfers between devices  72.3 us (16%)
  matrix products  23.6 us (5%)
  between operations  14.1 us (3%)
    psum x1, blocking collectives, body(): rot_rows = lax.psum(partial_grad, 'out').astype(jnp.bfloat16)  215 us
    psum x1, blocking collectives, body(): scores = lax.psum(partial_scores, ('loop', 'out')) / (KS * DIN) ** 0.5  101 us
    all_gather x1, waiting for transfers between devices, body(): grads_all = lax.all_gather(out_grads, 'loop', axis=1, tiled=True)  70.9 us
    all_gather x1, blocking collectives, body(): rot_act = lax.all_gather(rotated, 'loop', axis=1, tiled=True)  31.7 us
    dot_general x1, matrix products, body(): jnp.einsum('qcd,fcd->qf', scaled.astype(jnp.float32), grad_rot[queries:],...  12 us
  transfers between devices with their start and end apart: 2, of which 1 were waited for; matrix products, arithmetic and copies ran while one was open for 2% of the time, Pallas kernels for 0%

commit v1 on v0

--- a/solution.py
+++ b/solution.py
@@ -43,7 +43,7 @@
         grad_rot[queries:],
         precision=lax.Precision.HIGHEST,
     )
-    scores = lax.psum(partial_scores, ("loop", "out")) / (KS * DIN) ** 0.5
+    scores = lax.psum(lax.psum(partial_scores, "out"), "loop") / (KS * DIN) ** 0.5
     return (scaled, scores)
 
 

time: 460 us -> 453 us (0.985)
  blocking collectives: 347 us -> 340 us
    psum x1 -> x2, blocking collectives: 101 us -> 94.9 us  [the longest x1 48.2 us: body(): lax.psum(partial_scores, 'out')]
where the time goes in v1:
time: 453 us
  blocking collectives  340 us (75%)
  waiting for transfers between devices  72.3 us (16%)
  matrix products  23.6 us (5%)
  between operations  14.1 us (3%)
    psum x1, blocking collectives, body(): rot_rows = lax.psum(partial_grad, 'out').astype(jnp.bfloat16)  214 us
    all_gather x1, waiting for transfers between devices, body(): grads_all = lax.all_gather(out_grads, 'loop', axis=1, tiled=True)  70.9 us
    psum x1, blocking collectives, body(): lax.psum(partial_scores, 'out')  48.2 us
    psum x1, blocking collectives, body(): lax.psum(lax.psum(partial_scores, 'out'), 'loop') / (KS * DIN) ** 0.5  46.6 us
    all_gather x1, blocking collectives, body(): rot_act = lax.all_gather(rotated, 'loop', axis=1, tiled=True)  30.3 us
    dot_general x1, matrix products, body(): jnp.einsum('qcd,fcd->qf', scaled.astype(jnp.float32), grad_rot[queries:],...  12 us
  transfers between devices with their start and end apart: 2, of which 1 were waited for; matrix products, arithmetic and copies ran while one was open for 2% of the time, Pallas kernels for 0%

profile of v1, /device:TPU:1, one launch (start us, length us, event | category | flops | bytes accessed | tf_op | source)
XLA Modules:
  0.0 453.0 jit_solution(3222257674751457805)
XLA Ops:
  7.2 0.0 copy-start
  7.2 0.0 all-gather.3.cloned.1.call-start
  7.2 0.7 all-gather.3.cloned.1.call-update
  7.9 0.0 all-gather.5.cloned.1.call-start
  8.0 0.7 all-gather.5.cloned.1.call-update
  8.7 0.7 fusion.17
  9.4 1.3 broadcast_add_fusion
  10.7 70.9 %all-gather.3.cloned.1.call-done = bf16[10,128,896]{2,1,0:T(8,128)(2,1)} async-done(((bf16[10,8,896]{2,1,0:T(8,128)(2,1)}), bf16[10,128,896]{2,1,0:T(8,128)(2,1)}) %all-gather.3.cloned.1.call-update) | async-done | bytes 2293776 | tf_op jit(solution)/shard_map/all_gather | solution.py:26
  81.5 0.0 copy-done
  81.6 6.5 %fusion.18 = f32[1280,896]{1,0:T(8,128)} fusion(bf16[1280,896]{1,0:T(8,128)(2,1)} %bitcast.18, bf16[896,896]{1,0:T(8,128)(2,1)S(1)} %copy-done), kind=kOutput, calls=%fused_computation.17 | convolution fusion | flops 2055208960 | bytes 8486912 | tf_op jit(solution)/shard_map/dot_general | solution.py:28
  88.1 214.5 %all-reduce.1 = bf16[1280,896]{1,0:T(8,128)(2,1)} all-reduce(f32[1280,896]{1,0:T(8,128)} %fusion.18), channel_id=1, replica_groups=mesh['loop'=16,'out'=32] {'out'}, use_global_device_ids=true, to_apply=%region_0.0 | all-reduce | flops 1146880 | bytes 6881280 | tf_op jit(solution)/shard_map/psum | solution.py:29
  302.6 0.0 all-gather.5.cloned.1.call-done
  302.6 0.0 copy-start.1
  302.6 3.6 fusion.8
  306.1 30.3 %all_gather.11 = bf16[10,128,256]{2,1,0:T(8,128)(2,1)S(1)} all-gather(bf16[10,8,256]{2,1,0:T(8,128)(2,1)S(1)} %fusion.8), channel_id=1, replica_groups=mesh['loop'=16,'out'=32] {'loop'}, dimensions={1}, use_global_device_ids=true | all-gather | bytes 696320 | tf_op jit(solution)/shard_map/all_gather | solution.py:25
  336.5 0.0 copy-done.1
  336.5 1.4 broadcast_multiply_fusion
  337.9 0.5 slice.9
  338.4 0.2 fusion.2
  338.7 0.0 copy-start.2
  338.7 12.0 %fusion.11 = f32[2,8]{1,0:T(2,128)S(1)} fusion(f32[8,896,256]{2,1,0:T(8,128)S(1)} %slice.9, bf16[2,896,256]{2,1,0:T(8,128)(2,1)S(1)} %fusion.2), kind=kOutput, calls=%fused_computation.9 | convolution fusion | flops 44040192 | bytes 8257600 | tf_op jit(solution)/shard_map/qcd,fcd->qf/dot_general | solution.py:40
  350.7 0.0 copy-done.2
  350.7 48.2 %psum.22 = f32[2,8]{1,0:T(2,128)S(1)} all-reduce(f32[2,8]{1,0:T(2,128)S(1)} %fusion.11), channel_id=1, replica_groups=mesh['loop'=16,'out'=32] {'out'}, use_global_device_ids=true, to_apply=%region_1.0 | all-reduce | flops 16 | bytes 128 | tf_op jit(solution)/shard_map/psum | solution.py:46
  398.9 46.6 %psum.23 = f32[2,8]{1,0:T(2,128)S(1)} all-reduce(f32[2,8]{1,0:T(2,128)S(1)} %psum.22), channel_id=1, replica_groups=mesh['loop'=16,'out'=32] {'loop'}, use_global_device_ids=true, to_apply=%region_2.0 | all-reduce | flops 16 | bytes 128 | tf_op jit(solution)/shard_map/psum | solution.py:46
  445.6 0.6 broadcast_multiply_fusion.1
Async XLA Ops:
  7.2 74.4 %copy-start = (bf16[896,896]{1,0:T(8,128)(2,1)S(1)}, bf16[896,896]{1,0:T(8,128)(2,1)}, u32[]{:S(2)}) copy-start(bf16[896,896]{1,0:T(8,128)(2,1)} %param.10) | copy-start | bytes 4816900
  7.2 74.4 %all-gather.3.cloned.1.call-start = ((), (), s32[]{:S(2)}) async-start(), calls=%async_computation | async-start | bytes 2437120 | tf_op jit(solution)/shard_map/all_gather | solution.py:26
  7.9 294.6 %all-gather.5.cloned.1.call-start = ((), (), s32[]{:S(2)}) async-start(), calls=%async_computation.1 | async-start | bytes 4456448 | tf_op jit(solution)/shard_map/all_gather | solution.py:21
  302.6 33.9 %copy-start.1 = (bf16[1280,896]{1,0:T(8,128)(2,1)S(1)}, bf16[1280,896]{1,0:T(8,128)(2,1)}, u32[]{:S(2)}) copy-start(bf16[1280,896]{1,0:T(8,128)(2,1)} %all-reduce.1) | copy-start | bytes 6881284
  338.7 12.0 %copy-start.2 = (bf16[2,896,256]{2,1,0:T(8,128)(2,1)}, bf16[2,896,256]{2,1,0:T(8,128)(2,1)S(1)}, u32[]{:S(2)}) copy-start(bf16[2,896,256]{2,1,0:T(8,128)(2,1)S(1)} %fusion.2) | copy-start | bytes 2752516
Sparse Core Ops, SparseCore 0:
  11.4 70.1 all-gather.2
  84.8 97.8 all-gather.4
